TPU v7x, 32 devices: a whole 2x2x4 slice. The times are simulated.
32 devices in a mesh: row: 4 (over x, core), col: 8 (over z, y).
Axes of the slice: x: 2, y: 2, z: 4, core: 2. Of those that a mesh axis runs over, the one named last changes fastest.
Arguments:
- raw_vectors: float32 [2048, 81920], P('col', 'row'), may hold values from -810 to 810
- interval_count: int32 [8], replicated, may hold values from 1 to 256, 1024 in all
- cluster_of: int32 [8, 256], P('col'), may hold values from 0 to 31, never falling along the last dimension, each value on 1 to 32 neighbouring positions
- panel_one: float32 [81920, 256], P(('row', 'col')), may hold values from -0.03125 to 0.03125
- factor_one: float32 [256, 256], replicated, may hold values from -0.3 to 2
- panel_two: float32 [81920, 256], P(('row', 'col')), may hold values from -0.03125 to 0.03125
- factor_two: float32 [256, 256], replicated, may hold values from -0.3 to 2
Outputs:
- eigenvectors: float32 [1024, 81920], P('col', 'row')
Inputs may be any that keep to these rules, and one draw needn't show every extreme that they name: `interval_count`: the counts sum to 1024; one is exactly 256. `cluster_of`: labels never fall along an interval's slots; one label covers at most 32 slots, and one covers exactly 32.
All inputs are finite; a program needn't handle non-finite values.
Results may differ from a plain program's by a relative error of at most 0.0003.
Values sent between devices are 32-bit elements; how exact they have to be, the bound alone decides.
No kernel may reach another device: no remote copies, remote signals or barrier semaphores. Data moves between devices by JAX's collectives and lax.ppermute only.
A program may use at most 128 MiB of HBM per device.

v0:
```python
import math

import jax
import jax.numpy as jnp
from jax import lax
from jax.sharding import PartitionSpec as P

N = 81920
NB = 16
KD = 128


highest = lax.Precision.HIGHEST


def block_order(counts, column_count, per_device, capacity):
    positions = jnp.arange(column_count * per_device, dtype=jnp.int32)
    device_of = positions // per_device
    local_index = positions % per_device
    rank_of = (local_index // NB * column_count + device_of) * NB + local_index % NB
    interval_end = jnp.cumsum(counts)
    interval_start = interval_end - counts
    owner_device = jnp.sum((interval_end[None, :] <= rank_of[:, None]).astype(jnp.int32), axis=1)
    owner_hit = jnp.arange(column_count, dtype=jnp.int32)[None, :] == owner_device[:, None]
    owner_start = jnp.sum(jnp.where(owner_hit, interval_start[None, :], 0), axis=1)
    return owner_device * capacity + rank_of - owner_start


def finish_block(gram_full, raw_block, labels, is_alive):
    same_group = (labels[:, None] == labels[None, :]) & is_alive[:, None] & is_alive[None, :]
    alive_float = is_alive.astype(jnp.float32)
    masked = jnp.where(same_group, gram_full, 0.0) + jnp.diag(1.0 - alive_float)
    lower_factor = jnp.linalg.cholesky(masked)
    solved = jax.scipy.linalg.solve_triangular(lower_factor, raw_block, lower=True)
    return solved * math.sqrt(N)


def apply_panel(vectors, projected, reflectors, factor):
    scaled = jnp.dot(projected, factor.T, precision=highest, preferred_element_type=jnp.float32)
    return vectors - jnp.einsum("kr,nr->kn", scaled, reflectors, precision=highest)


def project_sum(partial_terms):
    return lax.psum(partial_terms, ("row", "col"))


def transform(vectors, reflect_one, factor_one, reflect_two, factor_two):
    for reflectors, factor in ((reflect_two, factor_two), (reflect_one, factor_one)):
        partial_terms = jnp.dot(
            vectors, reflectors, precision=highest, preferred_element_type=jnp.float32
        )
        projected = project_sum(partial_terms)
        vectors = apply_panel(vectors, projected, reflectors, factor)
    return vectors


def regroup(vectors):
    return lax.all_to_all(vectors, "col", split_axis=0, concat_axis=1, tiled=True)


def sectioned_order(orthogonal, interval_count, column_count, capacity):
    spread = lax.all_to_all(orthogonal, "col", split_axis=1, concat_axis=0, tiled=True)
    wanted = block_order(interval_count, column_count, KD, capacity)
    return jnp.take(spread, wanted, axis=0)


def body(raw_vectors, interval_count, cluster_of, panel_one, factor_one, panel_two, factor_two):
    column_count = lax.axis_size("col")
    column_index = lax.axis_index("col")
    capacity = raw_vectors.shape[0]
    own_hit = jnp.arange(column_count, dtype=jnp.int32) == column_index
    own_count = jnp.sum(jnp.where(own_hit, interval_count, 0))
    is_alive = jnp.arange(capacity, dtype=jnp.int32) < own_count
    gram_part = jnp.dot(
        raw_vectors, raw_vectors.T, precision=highest, preferred_element_type=jnp.float32
    )
    gram_full = lax.psum(gram_part, "row")
    orthogonal = finish_block(gram_full, raw_vectors, cluster_of[0], is_alive)
    ordered = sectioned_order(orthogonal, interval_count, column_count, capacity)
    return regroup(transform(ordered, panel_one, factor_one, panel_two, factor_two))


def solution(mesh):
    placed = (
        P("col", "row"),
        P(),
        P("col", None),
        P(("row", "col"), None),
        P(),
        P(("row", "col"), None),
        P(),
    )
    return jax.shard_map(
        body, mesh=mesh, in_specs=placed, out_specs=P("col", "row"), check_vma=False
    )
```

profile of v0, /device:TPU:8, one launch (start us, length us, event | category | flops | bytes accessed | tf_op | source)
XLA Modules:
  0.0 1239.1 jit_solution(12852142637741587065)
XLA Ops:
  6.5 22.9 %fusion.38 = f32[256,256]{0,1:T(8,128)} fusion(f32[256,20480]{1,0:T(8,128)} %param.7), kind=kOutput, calls=%fused_computation.95 | convolution fusion | flops 16106127360 | bytes 21233664 | tf_op jit(solution)/shard_map/dot_general | solution.py:74
  31.7 31.1 %all-reduce.5.cloned.1.call-done = f32[256,256]{0,1:T(8,128)} async-done(((f32[256,256]{0,1:T(8,128)}), f32[256,256]{0,1:T(8,128)}) %all-reduce.5.cloned.1.call-update) | async-done | bytes 262160 | tf_op jit(solution)/shard_map/psum | solution.py:77
  62.8 1.1 select_add_fusion
  64.0 1.1 fusion.7
  65.1 11.7 cholesky.49
  76.9 9.8 custom-call.15
  87.2 11.7 cholesky.103
  101.5 4.3 while.1
  102.1 1.4 dynamic-slice.7
  104.2 1.4 dynamic-slice.7
  105.8 20.2 %custom-call.16 = f32[2,128,128]{1,2,0:T(8,128)S(1)} custom-call(f32[2,128,128]{2,1,0:T(8,128)S(1)} %get-tuple-element.12), custom_call_target="InvertDiagBlocksLowerTriangular" | custom-call | tf_op jit(solution)/shard_map/jit(_solve_triangular)/triangular_solve | solution.py:34
  126.0 12.7 %fusion.1 = f32[128,20480]{1,0:T(8,128)S(1)} fusion(f32[256,20480]{1,0:T(8,128)} %param.7, f32[2,128,128]{1,2,0:T(8,128)S(1)} %custom-call.16), kind=kOutput, calls=%fused_computation.7 | convolution fusion | flops 4026531840 | bytes 21037056 | tf_op jit(solution)/shard_map/jit(_solve_triangular)/triangular_solve | solution.py:34
  138.7 4.0 copy-done.2
  142.7 13.4 %fusion = f32[20480,128]{0,1:T(8,128)} fusion(f32[128,20480]{1,0:T(8,128)S(1)} %fusion.1, f32[256,20480]{1,0:T(8,128)} %param.7, f32[256,256]{0,1:T(8,128)S(1)} %get-tuple-element.94), kind=kOutput, calls=%fused_computation.4 | convolution fusion | flops 4029153280 | bytes 31522816 | tf_op jit(solution)/shard_map/jit(_solve_triangular)/triangular_solve | solution.py:34
  156.0 11.9 copy.41
  167.9 17.6 %fusion.9 = f32[128,8,2560]{2,0,1:T(8,128)} fusion(f32[8,2560,128]{2,1,0:T(8,128)} %bitcast.67, f32[2,128,128]{1,2,0:T(8,128)S(1)} %custom-call.16), kind=kOutput, calls=%fused_computation.24 | convolution fusion | flops 4026531840 | bytes 21037056 | tf_op jit(solution)/shard_map/jit(_solve_triangular)/triangular_solve | solution.py:34
  185.5 5.0 copy.46
  190.5 17.2 %maximum_multiply_fusion = f32[256,8,2560]{2,0,1:T(8,128)} fusion(f32[128,8,2560]{2,0,1:T(8,128)} %fusion.9, f32[128,8,2560]{2,0,1:T(8,128)} %bitcast.66), kind=kLoop, calls=%fused_computation.5 | loop fusion | flops 10485760 | bytes 41943040 | tf_op jit(solution)/shard_map/mul | solution.py:35
  207.7 6.5 all-to-all-start
  214.5 448.9 %all-to-all-done = f32[256,8,2560]{2,0,1:T(8,128)} async-done(((f32[256,8,2560]{2,0,1:T(8,128)}), f32[256,8,2560]{2,0,1:T(8,128)}, u32[]{:S(2)}, u32[]{:S(2)}) %all-to-all-start) | async-done | bytes 20971552 | tf_op jit(solution)/shard_map/all_to_all | solution.py:62
  663.4 17.4 %gather_fusion = f32[1024,2560]{1,0:T(8,128)} fusion(f32[2048,2560]{1,0:T(8,128)} %bitcast.12, s32[1024]{0:T(1024)S(1)} %broadcast_clamp_fusion), kind=kCustom, calls=%fused_computation | custom fusion | bytes 20975616 | tf_op jit(solution)/shard_map/jit(_take)/gather | solution.py:64
  680.8 12.3 fusion.3
  693.2 130.7 %all-reduce.7.cloned.1.call-done = f32[1024,256]{1,0:T(8,128)} async-done(((f32[1024,256]{1,0:T(8,128)}), f32[1024,256]{1,0:T(8,128)}) %all-reduce.7.cloned.1.call-update) | async-done | bytes 1048592 | tf_op jit(solution)/shard_map/psum | solution.py:44
  823.8 2.2 fusion.39
  826.1 13.3 %select_subtract_fusion = f32[1024,2560]{1,0:T(8,128)S(1)} fusion(f32[1024,2560]{1,0:T(8,128)} %gather_fusion, f32[1024,256]{1,0:T(8,128)S(1)} %fusion.39, f32[2560,256]{1,0:T(8,128)S(1)} %copy-done, pred[1024]{0:T(1024)(128)(4,1)S(1)} %compare_and_fusion), kind=kOutput, calls=%fused_computation.9 | convolution fusion | flops 8058306560 | bytes 24642560 | tf_op jit(solution)/shard_map/kr,nr->kn/dot_general | solution.py:40
  839.4 4.1 copy-done.1
  843.5 9.3 fusion.40
  852.8 129.0 %all-reduce.9.cloned.1.call-done = f32[1024,256]{1,0:T(8,128)} async-done(((f32[1024,256]{1,0:T(8,128)}), f32[1024,256]{1,0:T(8,128)}) %all-reduce.9.cloned.1.call-update) | async-done | bytes 1048592 | tf_op jit(solution)/shard_map/psum | solution.py:44
  981.8 2.3 fusion.41
  984.1 13.0 %convolution_subtract_fusion.1 = f32[1024,2560]{1,0:T(8,128)S(1)} fusion(f32[1024,2560]{1,0:T(8,128)} %copy-done.1, f32[1024,256]{1,0:T(8,128)S(1)} %fusion.41, f32[2560,256]{1,0:T(8,128)} %param.10), kind=kOutput, calls=%fused_computation.12 | convolution fusion | flops 8055685120 | bytes 24641536 | tf_op jit(solution)/shard_map/kr,nr->kn/dot_general | solution.py:40
  997.1 230.2 %all_to_all.35 = f32[8,128,2560]{2,1,0:T(8,128)S(1)} all-to-all(f32[8,128,2560]{2,1,0:T(8,128)S(1)} %bitcast.68), channel_id=1, replica_groups=mesh['row'=4,'col'=8] {'col'}, dimensions={0} | all-to-all | bytes 20971520 | tf_op jit(solution)/shard_map/all_to_all | solution.py:58
  1227.3 5.1 copy.44
  (58 shorter events, 5.7 us)
Async XLA Ops:
  6.5 674.2 %copy-start = (f32[2560,256]{1,0:T(8,128)S(1)}, f32[2560,256]{1,0:T(8,128)}, u32[]{:S(2)}) copy-start(f32[2560,256]{1,0:T(8,128)} %param.12) | copy-start | bytes 7864324
  6.5 23.0 %copy-start.8 = (s32[8]{0:T(128)S(1)}, s32[8]{0:T(128)}, u32[]{:S(2)}) copy-start(s32[8]{0:T(128)} %param.8) | copy-start | bytes 100
  6.5 56.2 %copy-start.7 = (s32[1,256]{1,0:T(1,128)S(1)}, s32[1,256]{1,0:T(1,128)}, u32[]{:S(2)}) copy-start(s32[1,256]{1,0:T(1,128)} %param.9) | copy-start | bytes 3076
  6.5 56.2 %all-reduce.5.cloned.1.call-start = ((), (), s32[]{:S(2)}) async-start(), calls=%async_computation.2 | async-start | bytes 524288 | tf_op jit(solution)/shard_map/psum | solution.py:77
  138.7 4.0 copy-start.2
  167.9 17.6 %copy-start.3 = (f32[128,20480]{1,0:T(8,128)S(1)}, f32[128,20480]{1,0:T(8,128)}, u32[]{:S(2)}) copy-start(f32[128,20480]{1,0:T(8,128)} %copy-done.2) | copy-start | bytes 31457284
  207.7 455.7 %all-to-all-start = ((f32[256,8,2560]{2,0,1:T(8,128)}), f32[256,8,2560]{2,0,1:T(8,128)}, u32[]{:S(2)}, u32[]{:S(2)}) async-start(f32[256,8,2560]{2,0,1:T(8,128)} %maximum_multiply_fusion), calls=%async_computation | async-start | bytes 41943040 | tf_op jit(solution)/shard_map/all_to_all | solution.py:62
  214.2 609.6 %all-reduce.7.cloned.1.call-start = ((), (), s32[]{:S(2)}) async-start(), calls=%async_computation.3 | async-start | bytes 2097152 | tf_op jit(solution)/shard_map/psum | solution.py:44
  680.8 143.1 %copy-start.5 = (f32[256,256]{1,0:T(8,128)S(1)}, f32[256,256]{1,0:T(8,128)}, u32[]{:S(2)}) copy-start(f32[256,256]{1,0:T(8,128)} %param.13) | copy-start | bytes 786436
  693.1 288.7 %all-reduce.9.cloned.1.call-start = ((), (), s32[]{:S(2)}) async-start(), calls=%async_computation.4 | async-start | bytes 2097152 | tf_op jit(solution)/shard_map/psum | solution.py:44
  826.1 17.4 %copy-start.4 = (f32[2560,256]{1,0:T(8,128)S(1)}, f32[2560,256]{1,0:T(8,128)}, u32[]{:S(2)}) copy-start(f32[2560,256]{1,0:T(8,128)} %param.10) | copy-start | bytes 7864324
  839.4 4.1 copy-start.1
  843.5 138.3 %copy-start.6 = (f32[256,256]{1,0:T(8,128)S(1)}, f32[256,256]{1,0:T(8,128)}, u32[]{:S(2)}) copy-start(f32[256,256]{1,0:T(8,128)} %param.11) | copy-start | bytes 786436
Sparse Core Ops, SparseCore 0:
  29.6 33.1 all-reduce.4
  693.2 130.5 all-reduce.6
  852.9 128.7 all-reduce.8
where the time goes:
time: 1240 us
  waiting for transfers between devices  740 us (60%)
  blocking collectives  230 us (19%)
  matrix products  119 us (10%)
  other arithmetic  76 us (6%)
  local copies, waits for them, and re-layouts  52.2 us (4%)
  between operations  14.9 us (1%)
    all_to_all x1, waiting for transfers between devices, sectioned_order(): lax.all_to_all(orthogonal, 'col', split_axis=1, concat_axis=0, tiled=True)  449 us
    psum x2, waiting for transfers between devices, project_sum(): return lax.psum(partial_terms, ('row', 'col'))  260 us
    all_to_all x1, blocking collectives, regroup(): lax.all_to_all(vectors, 'col', split_axis=0, concat_axis=1, tiled=True)  230 us
    another operation x3, matrix products, finish_block(): jax.scipy.linalg.solve_triangular(lower_factor, raw_block, lower=True)  43.6 us
    another operation x6, other arithmetic, finish_block(): lower_factor = jnp.linalg.cholesky(masked)  34 us
    psum x1, waiting for transfers between devices, body(): gram_full = lax.psum(gram_part, 'row')  31.1 us
    dot_general x2, matrix products, apply_panel(): jnp.einsum('kr,nr->kn', scaled, reflectors, precision=highest)  26.3 us
  transfers between devices with their start and end apart: 4, of which 4 were waited for; matrix products, arithmetic and copies ran while one was open for 0% of the time, Pallas kernels for 0%

commit v1 on v0

v1 whole, which is shorter than its diff:
```python
import functools
import math

import jax
import jax.numpy as jnp
from jax import lax
from jax.experimental import pallas as pl
from jax.experimental.pallas import tpu as pltpu
from jax.sharding import PartitionSpec as P

N = 81920
NB = 16
KD = 128

highest = lax.Precision.HIGHEST


def dot_highest(a, b):
    return jnp.dot(a, b, precision=highest, preferred_element_type=jnp.float32)


def split_bf16(x):
    high = lax.reduce_precision(x, exponent_bits=8, mantissa_bits=7)
    return high.astype(jnp.bfloat16), (x - high).astype(jnp.bfloat16)


def swap(x, axis, step):
    size = lax.axis_size(axis)
    return lax.ppermute(x, axis, [(i, i ^ step) for i in range(size)])


def scatter_sum(x, axis, steps, index, unit):
    rows = x.shape[0] // (len(steps) + 1)
    total = lax.dynamic_slice_in_dim(x, index * rows, rows, 0)
    for step in steps:
        part = lax.dynamic_slice_in_dim(x, (index ^ step) * rows, rows, 0)
        total = total + swap(part, axis, step * unit)
    return total


def gather_rows(x, axis, steps, index, unit):
    rows = x.shape[0]
    whole = jnp.zeros(((len(steps) + 1) * rows,) + x.shape[1:], x.dtype)
    whole = lax.dynamic_update_slice_in_dim(whole, x, index * rows, 0)
    for step in steps:
        whole = lax.dynamic_update_slice_in_dim(whole, swap(x, axis, step * unit), (index ^ step) * rows, 0)
    return whole


def sum_everywhere(x):
    row_index, col_index = lax.axis_index("row"), lax.axis_index("col")
    stages = (
        ("row", range(1, 2), row_index % 2, 1),
        ("row", range(1, lax.axis_size("row") // 2), row_index // 2, 2),
        ("col", range(1, lax.axis_size("col")), col_index, 1),
    )
    for axis, steps, index, unit in stages:
        x = scatter_sum(x, axis, steps, index, unit)
    for axis, steps, index, unit in reversed(stages):
        x = gather_rows(x, axis, steps, index, unit)
    return x


def inverse_factor(gram_full, labels, is_alive):
    same_group = (labels[:, None] == labels[None, :]) & is_alive[:, None] & is_alive[None, :]
    alive_float = is_alive.astype(jnp.float32)
    masked = jnp.where(same_group, gram_full, 0.0) + jnp.diag(1.0 - alive_float)
    lower_factor = jnp.linalg.cholesky(masked)
    scaled_eye = math.sqrt(N) * jnp.eye(masked.shape[0], dtype=jnp.float32)
    return jax.scipy.linalg.solve_triangular(lower_factor, scaled_eye, lower=True)


def orthogonal_kernel(count, active_ref, owner_ref, factor_ref, high_ref, low_ref, *refs):
    blocks, ordered_ref, projected_ref, total = refs[:count], refs[count], refs[count + 1], refs[count + 2]
    window = NB * count

    @pl.when(pl.program_id(0) == 0)
    def _():
        projected_ref[...] = jnp.zeros_like(projected_ref)

    def one_window(j, carry):
        ranks = pl.ds(pl.multiple_of(j * window, window), window)
        local = pl.ds(pl.multiple_of(j * NB, NB), NB)
        total[...] = jnp.zeros_like(total)
        for k in range(count):

            @pl.when(active_ref[k, j] > 0)
            def _():
                factor = jnp.where(owner_ref[ranks, :] == k, factor_ref[ranks, :], 0.0)
                total[...] += dot_highest(factor, blocks[k][...])

        value = total[...]
        ordered_ref[:, local, :] = value.reshape(count, NB, value.shape[1])
        high = value.astype(jnp.bfloat16)
        low = (value - high.astype(jnp.float32)).astype(jnp.bfloat16)
        part = jnp.dot(high, high_ref[...], preferred_element_type=jnp.float32)
        part += jnp.dot(low, high_ref[...], preferred_element_type=jnp.float32)
        part += jnp.dot(high, low_ref[...], preferred_element_type=jnp.float32)
        projected_ref[:, local, :] += part.reshape(count, NB, part.shape[1])
        return carry

    lax.fori_loop(0, KD // NB, one_window, 0)


def orthogonalize(active, owner, factors, high, low, blocks):
    count, (capacity, width) = len(blocks), blocks[0].shape
    rank_total, reflectors = factors.shape[0], high.shape[1]
    tile = max(t for t in (128, 256, 512) if width % t == 0)
    whole = lambda shape: pl.BlockSpec(shape, lambda n, active: (0,) * len(shape))
    return pl.pallas_call(
        functools.partial(orthogonal_kernel, count),
        grid_spec=pltpu.PrefetchScalarGridSpec(
            num_scalar_prefetch=1,
            grid=(width // tile,),
            in_specs=[whole((rank_total, 1)), whole((rank_total, capacity))]
            + [pl.BlockSpec((tile, reflectors), lambda n, active: (n, 0))] * 2
            + [pl.BlockSpec((capacity, tile), lambda n, active: (0, n))] * count,
            out_specs=[
                pl.BlockSpec((count, KD, tile), lambda n, active: (0, 0, n)),
                whole((count, KD, reflectors)),
            ],
            scratch_shapes=[pltpu.VMEM((NB * count, tile), jnp.float32)],
        ),
        out_shape=[
            jax.ShapeDtypeStruct((count, KD, width), jnp.float32),
            jax.ShapeDtypeStruct((count, KD, reflectors), jnp.float32),
        ],
        compiler_params=pltpu.CompilerParams(vmem_limit_bytes=48 * 2**20),
    )(active, owner, factors, high, low, *blocks)


def body(raw_vectors, interval_count, cluster_of, panel_one, factor_one, panel_two, factor_two):
    column_count = lax.axis_size("col")
    column_index = lax.axis_index("col")
    capacity = raw_vectors.shape[0]
    width = panel_one.shape[0]
    columns = jnp.arange(column_count, dtype=jnp.int32)

    def column_block(k):
        return lax.dynamic_slice_in_dim(raw_vectors, (column_index ^ k) * width, width, 1)

    blocks = [column_block(0)] + [swap(column_block(k), "col", k) for k in range(1, column_count)]

    own_count = jnp.sum(jnp.where(columns == column_index, interval_count, 0))
    is_alive = jnp.arange(capacity, dtype=jnp.int32) < own_count
    gram_full = lax.psum(dot_highest(raw_vectors, raw_vectors.T), "row")
    inverse = inverse_factor(gram_full, cluster_of[0], is_alive)
    inverses = lax.all_gather(inverse, "col", axis=0, tiled=True)

    ranks = jnp.arange(column_count * KD, dtype=jnp.int32)
    interval_end = jnp.cumsum(interval_count).astype(jnp.int32)
    interval_start = interval_end - interval_count
    owner = jnp.sum((interval_end[None, :] <= ranks[:, None]).astype(jnp.int32), axis=1)
    owner_start = jnp.sum(jnp.where(columns[None, :] == owner[:, None], interval_start[None, :], 0), axis=1)
    factors = jnp.take(inverses, owner * capacity + ranks - owner_start, axis=0)
    window = NB * column_count
    window_start = jnp.arange(KD // NB, dtype=jnp.int32) * window
    overlap = (interval_start[:, None] < window_start[None, :] + window) & (
        interval_end[:, None] > window_start[None, :]
    )
    active = jnp.take(overlap.astype(jnp.int32), columns ^ column_index, axis=0)

    cross = lax.psum(dot_highest(panel_two.T, panel_one), ("row", "col"))
    weight_one = dot_highest(factor_one.T, panel_one.T)
    weight_two = dot_highest(factor_two.T, panel_two.T - dot_highest(cross, weight_one))
    weights = jnp.concatenate([weight_two, weight_one], axis=0)
    high, low = split_bf16(jnp.concatenate([panel_two, panel_one], axis=1))

    ordered, projected = orthogonalize(active, (owner ^ column_index)[:, None], factors, high, low, blocks)
    projected = sum_everywhere(projected.reshape(column_count * KD, -1))
    ordered = ordered.reshape(column_count * KD, width)
    result = ordered - jnp.dot(
        projected, weights, precision=lax.Precision.HIGH, preferred_element_type=jnp.float32
    )

    def row_block(k):
        return lax.dynamic_slice_in_dim(result, (column_index ^ k) * KD, KD, 0)

    gathered = jnp.zeros((KD, column_count * width), jnp.float32)
    for k in range(column_count):
        piece = swap(row_block(k), "col", k) if k else row_block(0)
        gathered = lax.dynamic_update_slice_in_dim(gathered, piece, (column_index ^ k) * width, 1)
    return gathered


def solution(mesh):
    placed = (
        P("col", "row"),
        P(),
        P("col", None),
        P(("row", "col"), None),
        P(),
        P(("row", "col"), None),
        P(),
    )
    return jax.shard_map(
        body, mesh=mesh, in_specs=placed, out_specs=P("col", "row"), check_vma=False
    )
```

time: 1240 us -> 1020 us (0.82)
  blocking collectives: 230 us -> 0 us
  matrix products: 119 us -> 57.3 us
  Pallas kernels: 0 us -> 56.1 us
  starting transfers between devices: 6.58 us -> 40.8 us
  waiting for transfers between devices: 740 us -> 715 us
    all_to_all x1 -> x0, waiting for transfers between devices: 449 us -> none  [sectioned_order(): lax.all_to_all(orthogonal, 'col', split_axis=1, concat_axis=0, tiled=True)]
    ppermute x0 -> x32, waiting for transfers between devices: none -> 376 us  [swap(): return lax.ppermute(x, axis, [(i, i ^ step) for i in range(size)])]
    all_to_all x1 -> x0, blocking collectives: 230 us -> none  [regroup(): lax.all_to_all(vectors, 'col', split_axis=0, concat_axis=1, tiled=True)]
    all_gather x0 -> x1, waiting for transfers between devices: none -> 202 us  [body(): inverses = lax.all_gather(inverse, 'col', axis=0, tiled=True)]
    psum x3 -> x2, waiting for transfers between devices: 291 us -> 137 us  [the longest x1 108 us: body(): cross = lax.psum(dot_highest(panel_two.T, panel_one), ('row', 'col'))]
    pallas_call x0 -> x1, Pallas kernels: none -> 56.1 us  [orthogonalize(): pl.pallas_call(functools.partial(orthogonal_kernel, count), grid_spec=plt...]
    another operation x5, matrix products: 44.1 us -> 3.29 us  [the longest x3 2.82 us: inverse_factor(): jax.scipy.linalg.solve_triangular(lower_factor, scaled_eye, lower=True)]
    ppermute x0 -> x32, starting transfers between devices: none -> 40.5 us  [swap(): return lax.ppermute(x, axis, [(i, i ^ step) for i in range(size)])]
  transfers between devices with their start and end apart: 4 -> 35, of which waited for: 4 -> 21; matrix products, arithmetic and copies ran while one was open for 0% -> 14% of each run, Pallas kernels for 0% -> 0%
where the time goes in v1:
time: 1020 us
  waiting for transfers between devices  715 us (70%)
  other arithmetic  68.4 us (7%)
  local copies, waits for them, and re-layouts  64.3 us (6%)
  matrix products  57.3 us (6%)
  Pallas kernels  56.1 us (6%)
  starting transfers between devices  40.8 us (4%)
  between operations  17 us (2%)
    ppermute x32, waiting for transfers between devices, swap(): return lax.ppermute(x, axis, [(i, i ^ step) for i in range(size)])  376 us
    all_gather x1, waiting for transfers between devices, body(): inverses = lax.all_gather(inverse, 'col', axis=0, tiled=True)  202 us
    psum x1, waiting for transfers between devices, body(): cross = lax.psum(dot_highest(panel_two.T, panel_one), ('row', 'col'))  108 us
    pallas_call x1, Pallas kernels, orthogonalize(): pl.pallas_call(functools.partial(orthogonal_kernel, count), grid_spec=plt...  56.1 us
    dot_general x5, matrix products, dot_highest(): return jnp.dot(a, b, precision=highest, preferred_element_type=jnp.float32)  42.2 us
    ppermute x32, starting transfers between devices, swap(): return lax.ppermute(x, axis, [(i, i ^ step) for i in range(size)])  40.5 us
    another operation x6, other arithmetic, inverse_factor(): lower_factor = jnp.linalg.cholesky(masked)  34 us
    psum x1, waiting for transfers between devices, body(): gram_full = lax.psum(dot_highest(raw_vectors, raw_vectors.T), 'row')  29.1 us
  transfers between devices with their start and end apart: 35, of which 21 were waited for; matrix products, arithmetic and copies ran while one was open for 14% of the time, Pallas kernels for 0%

profile of v1, /device:TPU:8, one launch (start us, length us, event | category | flops | bytes accessed | tf_op | source)
XLA Modules:
  0.0 1019.6 jit_solution(16563011858277407664)
XLA Ops:
  7.4 14.8 %constant_dynamic-slice_fusion.17 = (f32[256,2560]{1,0:T(8,128)}, f32[256,2560]{1,0:T(8,128)}, f32[256,2560]{1,0:T(8,128)}, f32[256,2560]{1,0:T(8,128)}, f32[256...) fusion(f32[256,20480]{1,0:T(8,128)} %param.7, s32[]{:T(128)S(6)} %select_n.194, ...), kind=kLoop, calls=%fused_computation.82 | loop fusion | bytes 41943072 | tf_op jit(solution)/shard_map/dynamic_slice | solution.py:140
  29.6 22.5 %fusion.20 = f32[256,256]{0,1:T(8,128)} fusion(f32[256,20480]{1,0:T(8,128)} %param.7), kind=kOutput, calls=%fused_computation.119 | convolution fusion | flops 16106127360 | bytes 21233664 | tf_op jit(solution)/shard_map/dot_general | solution.py:19
  55.4 29.1 %all-reduce.4.cloned.1.call-done = f32[256,256]{0,1:T(8,128)} async-done(((f32[256,256]{0,1:T(8,128)}), f32[256,256]{0,1:T(8,128)}) %all-reduce.4.cloned.1.call-update) | async-done | bytes 262160 | tf_op jit(solution)/shard_map/psum | solution.py:146
  86.9 11.7 %cholesky.49 = f32[128,128]{1,0:T(8,128)S(1)} custom-call(f32[128,128]{1,0:T(8,128)S(1)} %cholesky.115), custom_call_target="Cholesky" | custom-call | tf_op jit(solution)/shard_map/jit(cholesky)/cholesky | solution.py:68
  98.6 9.8 custom-call.15
  108.9 11.7 %cholesky.103 = f32[128,128]{1,0:T(8,128)S(1)} custom-call(f32[128,128]{1,0:T(8,128)S(1)} %convolution_subtract_fusion.2), custom_call_target="Cholesky" | custom-call | tf_op jit(solution)/shard_map/jit(cholesky)/cholesky | solution.py:68
  123.2 5.9 while.1
  129.0 20.5 %custom-call.16 = f32[2,128,128]{1,2,0:T(8,128)S(1)} custom-call(f32[2,128,128]{2,1,0:T(8,128)} %get-tuple-element.16), custom_call_target="InvertDiagBlocksLowerTriangular" | custom-call | tf_op jit(solution)/shard_map/jit(_solve_triangular)/triangular_solve | solution.py:70
  155.8 43.3 %collective-permute-done.1.refs_2_ = f32[256,2560]{1,0:T(8,128)} collective-permute-done((f32[256,2560]{1,0:T(8,128)}, f32[256,2560]{1,0:T(8,128)}, u32[]{:S(2)}, u32[]{:S(2)}) %collective-permute-start.1) | collective-permute-done | bytes 2621472 | tf_op jit(solution)/shard_map/ppermute | solution.py:29
  202.2 3.3 fusion
  205.5 202.1 %all-gather.2.cloned.1.call-done = f32[2048,256]{1,0:T(8,128)} async-done(((f32[256,256]{1,0:T(8,128)}), f32[2048,256]{1,0:T(8,128)}) %all-gather.2.cloned.1.call-update) | async-done | bytes 2097168 | tf_op jit(solution)/shard_map/all_gather | solution.py:148
  407.7 5.1 gather_fusion.1
  413.0 35.4 %collective-permute-done.5.refs_6_ = f32[256,2560]{1,0:T(8,128)} collective-permute-done((f32[256,2560]{1,0:T(8,128)}, f32[256,2560]{1,0:T(8,128)}, u32[]{:S(2)}, u32[]{:S(2)}) %collective-permute-start.5) | collective-permute-done | bytes 2621472 | tf_op jit(solution)/shard_map/ppermute | solution.py:29
  448.3 54.9 %collective-permute-done.6.refs_7_ = f32[256,2560]{1,0:T(8,128)} collective-permute-done((f32[256,2560]{1,0:T(8,128)}, f32[256,2560]{1,0:T(8,128)}, u32[]{:S(2)}, u32[]{:S(2)}) %collective-permute-start.6) | collective-permute-done | bytes 2621472 | tf_op jit(solution)/shard_map/ppermute | solution.py:29
  503.2 56.1 %shard_map.73 = (f32[8,128,2560]{2,1,0:T(8,128)}, f32[8,128,512]{2,1,0:T(8,128)S(1)}) custom-call(s32[8,8]{1,0:T(8,128)S(1)} %broadcast_select_fusion.1.active_ref, s32[1024,1]{1,0:T(8,128)S(1)} %copy.28.owner_ref, f32[1024,256]{1,0:T(8,128)S(1)} %broadcast_select_fusion.factor_ref, bf16[2560,512]{1,0:T(8,128)(2,1)} %get-tuple-element.58.high_ref, ...), custom_call_target="tpu_custom_call" | custom-call | tf_op jit(solution)/shard_map/pallas_call | solution.py:110
  560.4 3.0 collective-permute-done.7
  567.5 12.6 %collective-permute-done.8 = f32[256,512]{1,0:T(8,128)} collective-permute-done((f32[256,512]{1,0:T(8,128)S(1)}, f32[256,512]{1,0:T(8,128)}, u32[]{:S(2)}, u32[]{:S(2)}) %collective-permute-start.8) | collective-permute-done | bytes 524320 | tf_op jit(solution)/shard_map/ppermute | solution.py:29
  614.4 3.3 collective-permute-done.21
  620.7 6.7 fusion.21
  632.7 6.0 fusion.22
  638.8 3.4 copy.29
  642.2 108.3 %all-reduce.6.cloned.1.call-done = f32[256,256]{1,0:T(8,128)} async-done(((f32[256,256]{1,0:T(8,128)}), f32[256,256]{1,0:T(8,128)}) %all-reduce.6.cloned.1.call-update) | async-done | bytes 262160 | tf_op jit(solution)/shard_map/psum | solution.py:163
  750.5 4.3 convolution_subtract_fusion
  760.4 11.8 %bitcast_subtract_fusion = f32[1024,2560]{1,0:T(8,128)S(1)} fusion(f32[8,128,2560]{2,1,0:T(8,128)} %get-tuple-element.7, f32[1024,512]{1,0:T(8,128)S(1)} %constant_dynamic-update-slice_fusion.6, f32[256,2560]{1,0:T(8,128)S(1)} %fusion.22, f32[256,2560]{1,0:T(8,128)S(1)} %convolution_bitcast_fusion), kind=kOutput, calls=%fused_computation.4 | convolution fusion | flops 8056995840 | bytes 28311552 | tf_op jit(solution)/shard_map/dot_general | solution.py:172
  772.2 5.2 broadcast_in_dim.80
  777.3 3.3 constant_dynamic-slice_fusion.1
  787.9 23.4 %collective-permute-done.25 = f32[128,2560]{1,0:T(8,128)S(1)} collective-permute-done((f32[128,2560]{1,0:T(8,128)}, f32[128,2560]{1,0:T(8,128)S(1)}, u32[]{:S(2)}, u32[]{:S(2)}) %collective-permute-start.25) | collective-permute-done | bytes 1310752 | tf_op jit(solution)/shard_map/ppermute | solution.py:29
  813.3 52.6 %collective-permute-done.26 = f32[128,2560]{1,0:T(8,128)S(1)} collective-permute-done((f32[128,2560]{1,0:T(8,128)}, f32[128,2560]{1,0:T(8,128)S(1)}, u32[]{:S(2)}, u32[]{:S(2)}) %collective-permute-start.26) | collective-permute-done | bytes 1310752 | tf_op jit(solution)/shard_map/ppermute | solution.py:29
  867.8 24.0 %collective-permute-done.27 = f32[128,2560]{1,0:T(8,128)S(1)} collective-permute-done((f32[128,2560]{1,0:T(8,128)}, f32[128,2560]{1,0:T(8,128)S(1)}, u32[]{:S(2)}, u32[]{:S(2)}) %collective-permute-start.27) | collective-permute-done | bytes 1310752 | tf_op jit(solution)/shard_map/ppermute | solution.py:29
  894.1 61.4 %collective-permute-done.29 = f32[128,2560]{1,0:T(8,128)S(1)} collective-permute-done((f32[128,2560]{1,0:T(8,128)}, f32[128,2560]{1,0:T(8,128)S(1)}, u32[]{:S(2)}, u32[]{:S(2)}) %collective-permute-start.29) | collective-permute-done | bytes 1310752 | tf_op jit(solution)/shard_map/ppermute | solution.py:29
  956.7 27.9 %collective-permute-done.30 = f32[128,2560]{1,0:T(8,128)S(1)} collective-permute-done((f32[128,2560]{1,0:T(8,128)S(1)}, f32[128,2560]{1,0:T(8,128)S(1)}, u32[]{:S(2)}, u32[]{:S(2)}) %collective-permute-start.30) | collective-permute-done | bytes 1310752 | tf_op jit(solution)/shard_map/ppermute | solution.py:29
  985.7 25.1 %collective-permute-done.31 = f32[128,2560]{1,0:T(8,128)S(1)} collective-permute-done((f32[128,2560]{1,0:T(8,128)S(1)}, f32[128,2560]{1,0:T(8,128)S(1)}, u32[]{:S(2)}, u32[]{:S(2)}) %collective-permute-start.31) | collective-permute-done | bytes 1310752 | tf_op jit(solution)/shard_map/ppermute | solution.py:29
  (157 shorter events, 99.7 us)
Async XLA Ops:
  7.4 77.1 %all-reduce.4.cloned.1.call-start = ((), (), s32[]{:S(2)}) async-start(), calls=%async_computation | async-start | bytes 524288 | tf_op jit(solution)/shard_map/psum | solution.py:146
  22.2 132.0 %collective-permute-start = (f32[256,2560]{1,0:T(8,128)}, f32[256,2560]{1,0:T(8,128)S(1)}, u32[]{:S(2)}, u32[]{:S(2)}) collective-permute-start(f32[256,2560]{1,0:T(8,128)} %get-tuple-element.46), channel_id=1, source_target_pairs={{0,1},{1,0},{2,3},{3,2},{4,5},{5,4},{6,7},{7,6},{8,9},{9,8},{10,11... | collective-permute-start | bytes 7864328 | tf_op jit(solution)/shard_map/ppermute | solution.py:29
  23.8 175.3 %collective-permute-start.1 = (f32[256,2560]{1,0:T(8,128)}, f32[256,2560]{1,0:T(8,128)}, u32[]{:S(2)}, u32[]{:S(2)}) collective-permute-start(f32[256,2560]{1,0:T(8,128)} %get-tuple-element.45), channel_id=1, source_target_pairs={{0,2},{1,3},{2,0},{3,1},{4,6},{5,7},{6,4},{7,5},{8,10},{9,11},{10,... | collective-permute-start | bytes 7864328 | tf_op jit(solution)/shard_map/ppermute | solution.py:29
  24.2 388.7 %collective-permute-start.2 = (f32[256,2560]{1,0:T(8,128)}, f32[256,2560]{1,0:T(8,128)}, u32[]{:S(2)}, u32[]{:S(2)}) collective-permute-start(f32[256,2560]{1,0:T(8,128)} %get-tuple-element.44), channel_id=1, source_target_pairs={{0,3},{1,2},{2,1},{3,0},{4,7},{5,6},{6,5},{7,4},{8,11},{9,10},{10,... | collective-permute-start | bytes 7864328 | tf_op jit(solution)/shard_map/ppermute | solution.py:29
  25.8 387.2 %collective-permute-start.3 = (f32[256,2560]{1,0:T(8,128)}, f32[256,2560]{1,0:T(8,128)}, u32[]{:S(2)}, u32[]{:S(2)}) collective-permute-start(f32[256,2560]{1,0:T(8,128)} %get-tuple-element.43), channel_id=1, source_target_pairs={{0,4},{1,5},{2,6},{3,7},{4,0},{5,1},{6,2},{7,3},{8,12},{9,13},{10,... | collective-permute-start | bytes 7864328 | tf_op jit(solution)/shard_map/ppermute | solution.py:29
  28.3 384.6 %collective-permute-start.4 = (f32[256,2560]{1,0:T(8,128)}, f32[256,2560]{1,0:T(8,128)}, u32[]{:S(2)}, u32[]{:S(2)}) collective-permute-start(f32[256,2560]{1,0:T(8,128)} %get-tuple-element.42), channel_id=1, source_target_pairs={{0,5},{1,4},{2,7},{3,6},{4,1},{5,0},{6,3},{7,2},{8,13},{9,12},{10,... | collective-permute-start | bytes 7864328 | tf_op jit(solution)/shard_map/ppermute | solution.py:29
  52.2 355.5 %all-gather.2.cloned.1.call-start = ((), (), s32[]{:S(2)}) async-start(), calls=%async_computation.1 | async-start | bytes 2359296 | tf_op jit(solution)/shard_map/all_gather | solution.py:148
  153.1 597.4 %all-reduce.6.cloned.1.call-start = ((), (), s32[]{:S(2)}) async-start(), calls=%async_computation.2 | async-start | bytes 524288 | tf_op jit(solution)/shard_map/psum | solution.py:163
  154.2 294.1 %collective-permute-start.5 = (f32[256,2560]{1,0:T(8,128)}, f32[256,2560]{1,0:T(8,128)}, u32[]{:S(2)}, u32[]{:S(2)}) collective-permute-start(f32[256,2560]{1,0:T(8,128)} %get-tuple-element.48), channel_id=1, source_target_pairs={{0,6},{1,7},{2,4},{3,5},{4,2},{5,3},{6,0},{7,1},{8,14},{9,15},{10,... | collective-permute-start | bytes 7864328 | tf_op jit(solution)/shard_map/ppermute | solution.py:29
  199.1 304.2 %collective-permute-start.6 = (f32[256,2560]{1,0:T(8,128)}, f32[256,2560]{1,0:T(8,128)}, u32[]{:S(2)}, u32[]{:S(2)}) collective-permute-start(f32[256,2560]{1,0:T(8,128)} %get-tuple-element.41), channel_id=1, source_target_pairs={{0,7},{1,6},{2,5},{3,4},{4,3},{5,2},{6,1},{7,0},{8,15},{9,14},{10,... | collective-permute-start | bytes 7864328 | tf_op jit(solution)/shard_map/ppermute | solution.py:29
  565.9 14.1 %collective-permute-start.8 = (f32[256,512]{1,0:T(8,128)S(1)}, f32[256,512]{1,0:T(8,128)}, u32[]{:S(2)}, u32[]{:S(2)}) collective-permute-start(f32[256,512]{1,0:T(8,128)S(1)} %constant_dynamic-slice_fusion.15), channel_id=1, source_target_pairs={{0,16},{8,24},{16,0},{24,8},{1,17},{9,25},{17,1},{25,9},{2,18},{10... | collective-permute-start | bytes 1572872 | tf_op jit(solution)/shard_map/ppermute | solution.py:29
  582.1 8.6 collective-permute-start.10
  582.1 8.6 collective-permute-start.11
  584.3 8.1 collective-permute-start.12
  586.3 9.0 collective-permute-start.13
  587.9 9.6 collective-permute-start.14
  590.6 8.8 collective-permute-start.15
  590.7 8.8 collective-permute-start.9
  602.8 9.7 collective-permute-start.18
  605.4 7.8 collective-permute-start.19
  605.8 8.0 collective-permute-start.20
  608.7 9.1 collective-permute-start.21
  610.3 8.3 collective-permute-start.22
  619.2 12.7 %collective-permute-start.23 = (f32[256,512]{1,0:T(8,128)}, f32[256,512]{1,0:T(8,128)S(1)}, u32[]{:S(2)}, u32[]{:S(2)}) collective-permute-start(f32[256,512]{1,0:T(8,128)} %constant_dynamic-update-slice_fusion.10), channel_id=1, source_target_pairs={{0,16},{8,24},{16,0},{24,8},{1,17},{9,25},{17,1},{25,9},{2,18},{10... | collective-permute-start | bytes 1572872 | tf_op jit(solution)/shard_map/ppermute | solution.py:29
  632.7 126.3 %collective-permute-start.24 = (f32[512,512]{1,0:T(8,128)}, f32[512,512]{1,0:T(8,128)}, u32[]{:S(2)}, u32[]{:S(2)}) collective-permute-start(f32[512,512]{1,0:T(8,128)} %constant_dynamic-update-slice_fusion.8), channel_id=1, source_target_pairs={{0,8},{8,0},{16,24},{24,16},{1,9},{9,1},{17,25},{25,17},{2,10},{10... | collective-permute-start | bytes 3145736 | tf_op jit(solution)/shard_map/ppermute | solution.py:29
  780.6 30.8 %collective-permute-start.25 = (f32[128,2560]{1,0:T(8,128)}, f32[128,2560]{1,0:T(8,128)S(1)}, u32[]{:S(2)}, u32[]{:S(2)}) collective-permute-start(f32[128,2560]{1,0:T(8,128)} %get-tuple-element.55), channel_id=1, source_target_pairs={{0,1},{1,0},{2,3},{3,2},{4,5},{5,4},{6,7},{7,6},{8,9},{9,8},{10,11... | collective-permute-start | bytes 3932168 | tf_op jit(solution)/shard_map/ppermute | solution.py:29
  782.1 83.9 %collective-permute-start.26 = (f32[128,2560]{1,0:T(8,128)}, f32[128,2560]{1,0:T(8,128)S(1)}, u32[]{:S(2)}, u32[]{:S(2)}) collective-permute-start(f32[128,2560]{1,0:T(8,128)} %get-tuple-element.54), channel_id=1, source_target_pairs={{0,2},{1,3},{2,0},{3,1},{4,6},{5,7},{6,4},{7,5},{8,10},{9,11},{10,... | collective-permute-start | bytes 3932168 | tf_op jit(solution)/shard_map/ppermute | solution.py:29
  782.7 109.1 %collective-permute-start.27 = (f32[128,2560]{1,0:T(8,128)}, f32[128,2560]{1,0:T(8,128)S(1)}, u32[]{:S(2)}, u32[]{:S(2)}) collective-permute-start(f32[128,2560]{1,0:T(8,128)} %get-tuple-element.53), channel_id=1, source_target_pairs={{0,3},{1,2},{2,1},{3,0},{4,7},{5,6},{6,5},{7,4},{8,11},{9,10},{10,... | collective-permute-start | bytes 3932168 | tf_op jit(solution)/shard_map/ppermute | solution.py:29
  784.1 108.9 %collective-permute-start.28 = (f32[128,2560]{1,0:T(8,128)}, f32[128,2560]{1,0:T(8,128)S(1)}, u32[]{:S(2)}, u32[]{:S(2)}) collective-permute-start(f32[128,2560]{1,0:T(8,128)} %get-tuple-element.52), channel_id=1, source_target_pairs={{0,4},{1,5},{2,6},{3,7},{4,0},{5,1},{6,2},{7,3},{8,12},{9,13},{10,... | collective-permute-start | bytes 3932168 | tf_op jit(solution)/shard_map/ppermute | solution.py:29
  785.5 170.0 %collective-permute-start.29 = (f32[128,2560]{1,0:T(8,128)}, f32[128,2560]{1,0:T(8,128)S(1)}, u32[]{:S(2)}, u32[]{:S(2)}) collective-permute-start(f32[128,2560]{1,0:T(8,128)} %get-tuple-element.51), channel_id=1, source_target_pairs={{0,5},{1,4},{2,7},{3,6},{4,1},{5,0},{6,3},{7,2},{8,13},{9,12},{10,... | collective-permute-start | bytes 3932168 | tf_op jit(solution)/shard_map/ppermute | solution.py:29
  811.4 173.2 %collective-permute-start.30 = (f32[128,2560]{1,0:T(8,128)S(1)}, f32[128,2560]{1,0:T(8,128)S(1)}, u32[]{:S(2)}, u32[]{:S(2)}) collective-permute-start(f32[128,2560]{1,0:T(8,128)S(1)} %get-tuple-element.50), channel_id=1, source_target_pairs={{0,6},{1,7},{2,4},{3,5},{4,2},{5,3},{6,0},{7,1},{8,14},{9,15},{10,... | collective-permute-start | bytes 3932168 | tf_op jit(solution)/shard_map/ppermute | solution.py:29
  865.9 144.9 %collective-permute-start.31 = (f32[128,2560]{1,0:T(8,128)S(1)}, f32[128,2560]{1,0:T(8,128)S(1)}, u32[]{:S(2)}, u32[]{:S(2)}) collective-permute-start(f32[128,2560]{1,0:T(8,128)S(1)} %get-tuple-element.49), channel_id=1, source_target_pairs={{0,7},{1,6},{2,5},{3,4},{4,3},{5,2},{6,1},{7,0},{8,15},{9,14},{10,... | collective-permute-start | bytes 3932168 | tf_op jit(solution)/shard_map/ppermute | solution.py:29
  (11 other events, 939.0 us)
Sparse Core Ops, SparseCore 0:
  52.3 32.1 all-reduce.3
  153.2 254.3 all-gather.1
Sparse Core Ops, SparseCore 1:
  627.6 122.9 all-reduce.5

commit v2 on v1

v2 whole, which is shorter than its diff:
```python
import functools
import math

import jax
import jax.numpy as jnp
from jax import lax
from jax.experimental import pallas as pl
from jax.experimental.pallas import tpu as pltpu
from jax.sharding import PartitionSpec as P

N = 81920
NB = 16
KD = 128
CMAX = 32
STEP = 64

highest = lax.Precision.HIGHEST


def dot_highest(a, b):
    return jnp.dot(a, b, precision=highest, preferred_element_type=jnp.float32)


def split_bf16(x):
    high = lax.reduce_precision(x, exponent_bits=8, mantissa_bits=7)
    return high.astype(jnp.bfloat16), (x - high).astype(jnp.bfloat16)


def swap(x, axis, step):
    size = lax.axis_size(axis)
    return lax.ppermute(x, axis, [(i, i ^ step) for i in range(size)])


def scatter_sum(x, axis, steps, index, unit):
    rows = x.shape[0] // (len(steps) + 1)
    total = lax.dynamic_slice_in_dim(x, index * rows, rows, 0)
    for step in steps:
        part = lax.dynamic_slice_in_dim(x, (index ^ step) * rows, rows, 0)
        total = total + swap(part, axis, step * unit)
    return total


def gather_rows(x, axis, steps, index, unit):
    rows = x.shape[0]
    whole = jnp.zeros(((len(steps) + 1) * rows,) + x.shape[1:], x.dtype)
    whole = lax.dynamic_update_slice_in_dim(whole, x, index * rows, 0)
    for step in steps:
        whole = lax.dynamic_update_slice_in_dim(whole, swap(x, axis, step * unit), (index ^ step) * rows, 0)
    return whole


def sum_everywhere(x):
    row_index, col_index = lax.axis_index("row"), lax.axis_index("col")
    stages = (
        ("row", range(1, 2), row_index % 2, 1),
        ("row", range(1, lax.axis_size("row") // 2), row_index // 2, 2),
        ("col", range(1, lax.axis_size("col")), col_index, 1),
    )
    for axis, steps, index, unit in stages:
        x = scatter_sum(x, axis, steps, index, unit)
    for axis, steps, index, unit in reversed(stages):
        x = gather_rows(x, axis, steps, index, unit)
    return x


def inverse_factor(gram_full, labels, is_alive):
    same_group = (labels[:, None] == labels[None, :]) & is_alive[:, None] & is_alive[None, :]
    alive_float = is_alive.astype(jnp.float32)
    masked = jnp.where(same_group, gram_full, 0.0) + jnp.diag(1.0 - alive_float)
    lower_factor = jnp.linalg.cholesky(masked)
    scaled_eye = math.sqrt(N) * jnp.eye(masked.shape[0], dtype=jnp.float32)
    return jax.scipy.linalg.solve_triangular(lower_factor, scaled_eye, lower=True)


def take_band(inverse):
    padded = jnp.pad(inverse, ((0, 0), (CMAX, 0)))
    groups = range(0, inverse.shape[0], CMAX)
    return jnp.concatenate([padded[g : g + CMAX, g : g + 2 * CMAX] for g in groups], axis=0)


def spread_band(bands, capacity):
    bands = bands.reshape(-1, capacity, 2 * CMAX)
    groups = [
        jnp.pad(bands[:, g : g + CMAX], ((0, 0), (0, 0), (g, capacity - CMAX - g)))
        for g in range(0, capacity, CMAX)
    ]
    return jnp.concatenate(groups, axis=1)[:, :, CMAX:].reshape(-1, capacity)


def orthogonal_kernel(count, split, base_ref, owner_ref, factor_ref, high_ref, low_ref, *refs):
    blocks, rest = refs[:count], refs[count:]
    ordered_ref, projected_ref, total = rest[-3:]
    rank_total, capacity = ordered_ref.shape[0], factor_ref.shape[1]
    total[...] = jnp.zeros_like(total)
    for k in range(count):
        block = blocks[k][...]
        if split:
            begin = k % 2 * split
            beyond = rest[k][...] if k < 2 else rest[2][k // 2 - 1, begin : begin + split, :]
            block = jnp.concatenate([block, beyond], axis=0)
        block_high = block.astype(jnp.bfloat16)
        block_low = (block - block_high.astype(jnp.float32)).astype(jnp.bfloat16)
        ranks = pl.ds(pl.multiple_of(base_ref[k], 8), capacity + 2 * 8)
        factor = jnp.where(owner_ref[ranks, :] == k, factor_ref[ranks, :], 0.0)
        factor_high = factor.astype(jnp.bfloat16)
        factor_low = (factor - factor_high.astype(jnp.float32)).astype(jnp.bfloat16)
        part = jnp.dot(factor_high, block_high, preferred_element_type=jnp.float32)
        part += jnp.dot(factor_high, block_low, preferred_element_type=jnp.float32)
        part += jnp.dot(factor_low, block_high, preferred_element_type=jnp.float32)
        total[ranks, :] += part

    value = total[:rank_total, :]
    ordered_ref[...] = value
    value_high = value.astype(jnp.bfloat16)
    value_low = (value - value_high.astype(jnp.float32)).astype(jnp.bfloat16)
    projected = jnp.dot(value_high, high_ref[...], preferred_element_type=jnp.float32)
    projected += jnp.dot(value_low, high_ref[...], preferred_element_type=jnp.float32)
    projected += jnp.dot(value_high, low_ref[...], preferred_element_type=jnp.float32)

    @pl.when(pl.program_id(0) == 0)
    def _():
        projected_ref[...] = projected

    @pl.when(pl.program_id(0) > 0)
    def _():
        projected_ref[...] += projected


def orthogonalize(rank_total, base, owner, factors, high, low, blocks, excess):
    count, (rows, width) = len(blocks), blocks[0].shape
    reflectors, (padded, capacity) = high.shape[1], factors.shape
    tile = max(t for t in (128, 256, 512) if width % t == 0)
    whole = lambda shape: pl.BlockSpec(shape, lambda n, *_: (0,) * len(shape))
    column = lambda shape: pl.BlockSpec(shape + (tile,), lambda n, *_: (0,) * len(shape) + (n,))
    return pl.pallas_call(
        functools.partial(orthogonal_kernel, count, rows if excess else 0),
        grid_spec=pltpu.PrefetchScalarGridSpec(
            num_scalar_prefetch=1,
            grid=(width // tile,),
            in_specs=[whole((padded, 1)), whole((padded, capacity))]
            + [pl.BlockSpec((tile, reflectors), lambda n, *_: (n, 0))] * 2
            + [column((rows,))] * count
            + [column(e.shape[:-1]) for e in excess],
            out_specs=[column((rank_total,)), whole((rank_total, reflectors))],
            scratch_shapes=[pltpu.VMEM((padded, tile), jnp.float32)],
        ),
        out_shape=[
            jax.ShapeDtypeStruct((rank_total, width), jnp.float32),
            jax.ShapeDtypeStruct((rank_total, reflectors), jnp.float32),
        ],
        compiler_params=pltpu.CompilerParams(vmem_limit_bytes=56 * 2**20),
    )(base, owner, factors, high, low, *blocks, *excess)


def correct_kernel(count, target_ref, ordered_ref, projected_ref, weight_ref, *refs):
    pieces, high, low, result = refs[:count], refs[-3], refs[-2], refs[-1]

    @pl.when(pl.program_id(0) == 0)
    def _():
        projected = projected_ref[...]
        rounded = projected.astype(jnp.bfloat16)
        high[...] = rounded
        low[...] = (projected - rounded.astype(jnp.float32)).astype(jnp.bfloat16)

    weight = weight_ref[...]
    weight_high = weight.astype(jnp.bfloat16)
    weight_low = (weight - weight_high.astype(jnp.float32)).astype(jnp.bfloat16)
    product = jnp.dot(high[...], weight_high, preferred_element_type=jnp.float32)
    product += jnp.dot(low[...], weight_high, preferred_element_type=jnp.float32)
    product += jnp.dot(high[...], weight_low, preferred_element_type=jnp.float32)
    result[...] = ordered_ref[...] - product
    for k in range(count):
        for j in range(KD // NB):
            rows = pl.ds(pl.multiple_of((j * count + target_ref[k]) * NB, NB), NB)
            pieces[k][j * NB : (j + 1) * NB, :] = result[rows, :]


def correct(target, ordered, projected, weights):
    count, (rank_total, width), reflectors = target.shape[0], ordered.shape, weights.shape[0]
    tile = max(t for t in (128, 256, 512) if width % t == 0)
    column = lambda rows: pl.BlockSpec((rows, tile), lambda n, *_: (0, n))
    return pl.pallas_call(
        functools.partial(correct_kernel, count),
        grid_spec=pltpu.PrefetchScalarGridSpec(
            num_scalar_prefetch=1,
            grid=(width // tile,),
            in_specs=[
                column(rank_total),
                pl.BlockSpec((rank_total, reflectors), lambda n, *_: (0, 0)),
                column(reflectors),
            ],
            out_specs=[column(KD)] * count,
            scratch_shapes=[pltpu.VMEM((rank_total, reflectors), jnp.bfloat16)] * 2
            + [pltpu.VMEM((rank_total, tile), jnp.float32)],
        ),
        out_shape=[jax.ShapeDtypeStruct((KD, width), jnp.float32)] * count,
        compiler_params=pltpu.CompilerParams(vmem_limit_bytes=56 * 2**20),
    )(target, ordered, projected, weights)


def pair_excess(raw_vectors, half, width, pairs):
    column_index = lax.axis_index("col")
    parity = column_index % 2

    def side(which):
        cut = [
            lax.dynamic_slice(raw_vectors, (half, (2 * p + which) * width), (half, width)) for p in range(pairs)
        ]
        return jnp.stack(cut)

    first = lax.dynamic_slice(raw_vectors, (0, (column_index ^ 1) * width), (half, width))
    return side(parity), swap(jnp.concatenate([side(1 - parity), first[None]]), "col", 1)


def send_excess(own, other, beyond, pairs):
    pair_index, parity = lax.axis_index("col") // 2, lax.axis_index("col") % 2
    half, width = own.shape[1:]
    steps = (beyond.reshape(pairs, 2) + STEP - 1) // STEP
    own_steps = jnp.where(parity == 0, steps[:, 0], steps[:, 1])
    total_steps = jnp.sum(steps, axis=1)
    order = jnp.arange(pairs, dtype=jnp.int32)
    held = jnp.zeros((pairs - 1, 2 * half + STEP, width), jnp.float32)

    def branch(bits):
        def send(chunks):
            got = []
            for k in range(1, pairs):
                links = [(s, s ^ (2 * k)) for s in range(2 * pairs) if bits >> (s // 2) & 1]
                got.append(lax.ppermute(chunks[k - 1], "col", links) if links else chunks[k - 1])
            return got

        return send

    def step(carry):
        i, held = carry
        going = i < total_steps
        place = jnp.where(i < own_steps, i, half // STEP + i - own_steps)
        place = jnp.where(going, place, 2 * half // STEP) * STEP
        begin = jnp.sum(jnp.where(order == pair_index, place, 0))

        def chunk(k):
            from_own = lax.dynamic_slice(own, (pair_index ^ k, begin, 0), (1, STEP, width))
            from_other = lax.dynamic_slice(other, (pair_index ^ k, begin - half, 0), (1, STEP, width))
            return jnp.where(begin < half, from_own, from_other)

        bits = jnp.sum(jnp.where(going, 1 << order, 0))
        got = lax.switch(bits, [branch(b) for b in range(1 << pairs)], [chunk(k) for k in range(1, pairs)])
        for k in range(1, pairs):
            at = jnp.sum(jnp.where(order == (pair_index ^ k), place, 0))
            held = lax.dynamic_update_slice(held, got[k - 1], (k - 1, at, 0))
        return i + 1, held

    return lax.while_loop(lambda carry: carry[0] < jnp.max(total_steps), step, (jnp.int32(0), held))[1]


def body(raw_vectors, interval_count, cluster_of, panel_one, factor_one, panel_two, factor_two):
    column_count = lax.axis_size("col")
    column_index = lax.axis_index("col")
    capacity = raw_vectors.shape[0]
    width = panel_one.shape[0]
    rank_total = column_count * KD
    columns = jnp.arange(column_count, dtype=jnp.int32)
    pairs = column_count // 2
    balanced = pairs < 1
    half = capacity // 2
    sent_rows = half if balanced else capacity

    def column_block(k):
        return lax.dynamic_slice(raw_vectors, (0, (column_index ^ k) * width), (sent_rows, width))

    blocks = {0: column_block(0)}
    if balanced:
        own, other = pair_excess(raw_vectors, half, width, pairs)
        blocks[1] = other[pairs]
    for k in sorted(set(range(1, column_count)) - set(blocks), key=lambda k: (-(k.bit_length()), k & 1, k)):
        blocks[k] = swap(column_block(k), "col", k)
    blocks = [blocks[k] for k in range(column_count)]

    own_count = jnp.sum(jnp.where(columns == column_index, interval_count, 0))
    is_alive = jnp.arange(capacity, dtype=jnp.int32) < own_count
    gram_rows, left_panel, blocks[1] = lax.optimization_barrier((raw_vectors, panel_two, blocks[1]))
    gram_full = lax.psum(dot_highest(gram_rows, gram_rows.T), "row")
    cross = lax.psum(dot_highest(left_panel.T, panel_one), ("row", "col"))
    inverse = inverse_factor(gram_full, cluster_of[0], is_alive)
    inverses = spread_band(lax.all_gather(take_band(inverse), "col", axis=0, tiled=True), capacity)

    padded = rank_total + capacity + 2 * 8
    ranks = jnp.arange(padded, dtype=jnp.int32)
    interval_end = jnp.cumsum(interval_count).astype(jnp.int32)
    interval_start = interval_end - interval_count
    owner = jnp.sum((interval_end[None, :] <= ranks[:, None]).astype(jnp.int32), axis=1)
    owner_start = jnp.sum(jnp.where(columns[None, :] == owner[:, None], interval_start[None, :], 0), axis=1)
    slot = jnp.where(owner < column_count, owner * capacity + ranks - owner_start, 0)
    factors = jnp.take(inverses, slot, axis=0)
    factors, cross = lax.optimization_barrier((factors, cross))
    owner = jnp.where(owner < column_count, owner ^ column_index, -1)[:, None]
    base = jnp.take(interval_start // 8 * 8, columns ^ column_index)

    weight_one = dot_highest(factor_one.T, panel_one.T)
    weight_two = dot_highest(factor_two.T, panel_two.T - dot_highest(cross, weight_one))
    weights = jnp.concatenate([weight_two, weight_one], axis=0)
    high, low = split_bf16(jnp.concatenate([panel_two, panel_one], axis=1))

    excess = []
    if balanced:
        own, other, factors, weights, blocks = lax.optimization_barrier((own, other, factors, weights, blocks))
        mine = [lax.dynamic_index_in_dim(x, column_index // 2, 0, keepdims=False) for x in (own, other)]
        excess = mine + [send_excess(own, other, jnp.maximum(interval_count - half, 0), pairs)]

    ordered, projected = orthogonalize(rank_total, base, owner, factors, high, low, blocks, excess)
    pieces = correct(columns ^ column_index, ordered, sum_everywhere(projected), weights)
    gathered = jnp.zeros((KD, column_count * width), jnp.float32)
    for k in sorted(range(column_count), key=lambda k: (-(k.bit_length()), k & 1, k)):
        piece = swap(pieces[k], "col", k) if k else pieces[0]
        gathered = lax.dynamic_update_slice_in_dim(gathered, piece, (column_index ^ k) * width, 1)
    return gathered


def solution(mesh):
    placed = (
        P("col", "row"),
        P(),
        P("col", None),
        P(("row", "col"), None),
        P(),
        P(("row", "col"), None),
        P(),
    )
    return jax.shard_map(
        body, mesh=mesh, in_specs=placed, out_specs=P("col", "row"), check_vma=False
    )
```

time: 1020 us -> 896 us (0.88)
  waiting for transfers between devices: 715 us -> 310 us
  blocking collectives: 0 us -> 305 us
  matrix products: 57.3 us -> 41.9 us
  local copies, waits for them, and re-layouts: 64.3 us -> 49.6 us
  Pallas kernels: 56.1 us -> 44.4 us
    all_gather x0 -> x1, blocking collectives: none -> 305 us  [body(): lax.all_gather(take_band(inverse), 'col', axis=0, tiled=True)]
    all_gather x1 -> x0, waiting for transfers between devices: 202 us -> none  [body(): inverses = lax.all_gather(inverse, 'col', axis=0, tiled=True)]
    psum x2, waiting for transfers between devices: 137 us -> 25 us  [the longest x1 25 us: body(): gram_full = lax.psum(dot_highest(gram_rows, gram_rows.T), 'row')]
    ppermute x32, waiting for transfers between devices: 376 us -> 285 us  [swap(): return lax.ppermute(x, axis, [(i, i ^ step) for i in range(size)])]
    dot_general x1 -> x0, matrix products: 11.8 us -> none  [body(): jnp.dot(projected, weights, precision=lax.Precision.HIGH, preferred_eleme...]
    pallas_call x1 -> x2, Pallas kernels: 56.1 us -> 44.4 us  [the longest x1 28.7 us: orthogonalize(): pl.pallas_call(functools.partial(orthogonal_kernel, count, rows if excess...]
    another operation x4 -> x3, other arithmetic: 21.2 us -> 19.7 us  [inverse_factor(): jax.scipy.linalg.solve_triangular(lower_factor, scaled_eye, lower=True)]
  transfers between devices with their start and end apart: 35 -> 34, of which waited for: 21 -> 15; matrix products, arithmetic and copies ran while one was open for 14% -> 15% of each run, Pallas kernels for 0% -> 0%
where the time goes in v2:
time: 896 us; the launch traced here: 886 us
  waiting for transfers between devices  310 us (35%)
  blocking collectives  305 us (34%)
  other arithmetic  74.4 us (8%)
  local copies, waits for them, and re-layouts  49.6 us (6%)
  starting transfers between devices  45.1 us (5%)
  Pallas kernels  44.4 us (5%)
  matrix products  41.9 us (5%)
  between operations  15.5 us (2%)
    all_gather x1, blocking collectives, body(): lax.all_gather(take_band(inverse), 'col', axis=0, tiled=True)  305 us
    ppermute x32, waiting for transfers between devices, swap(): return lax.ppermute(x, axis, [(i, i ^ step) for i in range(size)])  285 us
    ppermute x32, starting transfers between devices, swap(): return lax.ppermute(x, axis, [(i, i ^ step) for i in range(size)])  44.9 us
    dot_general x5, matrix products, dot_highest(): return jnp.dot(a, b, precision=highest, preferred_element_type=jnp.float32)  40.4 us
    another operation x6, other arithmetic, inverse_factor(): lower_factor = jnp.linalg.cholesky(masked)  34.3 us
    pallas_call x1, Pallas kernels, orthogonalize(): pl.pallas_call(functools.partial(orthogonal_kernel, count, rows if excess...  28.7 us
    psum x1, waiting for transfers between devices, body(): gram_full = lax.psum(dot_highest(gram_rows, gram_rows.T), 'row')  25 us
    another operation x3, other arithmetic, inverse_factor(): jax.scipy.linalg.solve_triangular(lower_factor, scaled_eye, lower=True)  19.7 us
  transfers between devices with their start and end apart: 34, of which 15 were waited for; matrix products, arithmetic and copies ran while one was open for 15% of the time, Pallas kernels for 0%

profile of v2, /device:TPU:8, one launch (start us, length us, event | category | flops | bytes accessed | tf_op | source)
XLA Modules:
  0.0 886.3 jit_solution(6912685946095097643)
XLA Ops:
  6.5 15.0 %constant_dynamic-slice_fusion.10 = (f32[256,2560]{1,0:T(8,128)}, f32[256,2560]{1,0:T(8,128)}, f32[256,2560]{1,0:T(8,128)}, f32[256,2560]{1,0:T(8,128)}, f32[256...) fusion(f32[256,20480]{1,0:T(8,128)} %param.7, s32[]{:T(128)S(6)} %select_n.203, ...), kind=kLoop, calls=%fused_computation.95 | loop fusion | bytes 41943072 | tf_op jit(solution)/shard_map/dynamic_slice | solution.py:269
  36.5 3.3 fusion
  39.7 41.1 %collective-permute-done.refs_1_ = f32[256,2560]{1,0:T(8,128)} collective-permute-done((f32[256,2560]{1,0:T(8,128)}, f32[256,2560]{1,0:T(8,128)}, u32[]{:S(2)}, u32[]{:S(2)}) %collective-permute-start) | collective-permute-done | bytes 2621472 | tf_op jit(solution)/shard_map/ppermute | solution.py:31
  82.4 22.5 %fusion.17 = f32[256,256]{0,1:T(8,128)} fusion(f32[256,20480]{1,0:T(8,128)} %param.7), kind=kOutput, calls=%fused_computation.133 | convolution fusion | flops 16106127360 | bytes 21233664 | tf_op jit(solution)/shard_map/dot_general | solution.py:21
  105.1 6.7 fusion.18
  111.9 25.0 %all-reduce.13.cloned.1.call-done = f32[256,256]{0,1:T(8,128)} async-done(((f32[256,256]{0,1:T(8,128)}), f32[256,256]{0,1:T(8,128)}) %all-reduce.13.cloned.1.call-update) | async-done | bytes 262160 | tf_op jit(solution)/shard_map/psum | solution.py:282
  139.2 11.7 %cholesky.49 = f32[128,128]{1,0:T(8,128)S(1)} custom-call(f32[128,128]{1,0:T(8,128)S(1)} %cholesky.115), custom_call_target="Cholesky" | custom-call | tf_op jit(solution)/shard_map/jit(cholesky)/cholesky | solution.py:70
  151.0 9.8 %custom-call.15 = f32[1,128,128]{1,2,0:T(8,128)S(1)} custom-call(f32[1,128,128]{2,1,0:T(8,128)S(1)} %get-tuple-element.97), custom_call_target="InvertDiagBlocksLowerTriangular" | custom-call | tf_op jit(solution)/shard_map/jit(cholesky)/cholesky | solution.py:70
  161.3 12.1 %cholesky.103 = f32[128,128]{1,0:T(8,128)S(1)} custom-call(f32[128,128]{1,0:T(8,128)S(1)} %convolution_subtract_fusion.2), custom_call_target="Cholesky" | custom-call | tf_op jit(solution)/shard_map/jit(cholesky)/cholesky | solution.py:70
  175.7 4.0 while.1
  179.8 19.7 %custom-call.16 = f32[2,128,128]{1,2,0:T(8,128)S(1)} custom-call(f32[2,128,128]{2,1,0:T(8,128)S(1)} %get-tuple-element.42), custom_call_target="InvertDiagBlocksLowerTriangular" | custom-call | tf_op jit(solution)/shard_map/jit(_solve_triangular)/triangular_solve | solution.py:72
  203.3 305.4 %all_gather.3 = f32[2048,64]{1,0:T(8,128)S(1)} all-gather(f32[256,64]{1,0:T(8,128)S(1)} %constant_dynamic-update-slice_fusion), channel_id=1, replica_groups=mesh['row'=4,'col'=8] {'col'}, dimensions={0}, use_global_device_ids=true | all-gather | bytes 589824 | tf_op jit(solution)/shard_map/all_gather | solution.py:285
  510.4 4.6 gather_fusion.1
  515.0 2.6 broadcast_select_fusion.factor_ref
  517.7 28.7 %shard_map.73 = (f32[1024,2560]{1,0:T(8,128)}, f32[1024,512]{1,0:T(8,128)}) custom-call(s32[8]{0:T(128)} %and_select_fusion.1.base_ref, s32[1296,1]{1,0:T(8,128)} %reshape_select_fusion.owner_ref, f32[1296,256]{1,0:T(8,128)} %broadcast_select_fusion.factor_ref, bf16[2560,512]{1,0:T(8,128)(2,1)} %get-tuple-element.80.high_ref, ...), custom_call_target="tpu_custom_call" | custom-call | tf_op jit(solution)/shard_map/pallas_call | solution.py:135
  547.9 2.7 collective-permute-done.7
  554.7 12.6 %collective-permute-done.8 = f32[256,512]{1,0:T(8,128)} collective-permute-done((f32[256,512]{1,0:T(8,128)S(1)}, f32[256,512]{1,0:T(8,128)}, u32[]{:S(2)}, u32[]{:S(2)}) %collective-permute-start.8) | collective-permute-done | bytes 524320 | tf_op jit(solution)/shard_map/ppermute | solution.py:31
  572.4 2.8 collective-permute-start.13
  581.2 3.1 collective-permute-done.14
  588.9 2.8 collective-permute-start.18
  600.8 3.0 collective-permute-done.21
  609.5 6.1 fusion.19
  620.9 2.6 convolution_bitcast_fusion
  623.5 2.7 pad_maximum_fusion.weight_ref
  627.9 15.7 %shard_map.74 = (f32[128,2560]{1,0:T(8,128)}, f32[128,2560]{1,0:T(8,128)}, f32[128,2560]{1,0:T(8,128)}, f32[128,2560]{1,0:T(8,128)}, f32[128,2560]{1,0:T(8,128)}...) custom-call(s32[8]{0:T(128)} %iota_xor_fusion.target_ref, ...), custom_call_target="tpu_custom_call" | custom-call | tf_op jit(solution)/shard_map/pallas_call | solution.py:182
  645.2 3.7 collective-permute-start.27
  650.5 135.2 %collective-permute-done.25 = f32[128,2560]{1,0:T(8,128)S(1)} collective-permute-done((f32[128,2560]{1,0:T(8,128)}, f32[128,2560]{1,0:T(8,128)S(1)}, u32[]{:S(2)}, u32[]{:S(2)}) %collective-permute-start.25) | collective-permute-done | bytes 1310752 | tf_op jit(solution)/shard_map/ppermute | solution.py:31
  785.6 3.7 collective-permute-start.30
  790.5 25.0 %collective-permute-done.26 = f32[128,2560]{1,0:T(8,128)S(1)} collective-permute-done((f32[128,2560]{1,0:T(8,128)}, f32[128,2560]{1,0:T(8,128)S(1)}, u32[]{:S(2)}, u32[]{:S(2)}) %collective-permute-start.26) | collective-permute-done | bytes 1310752 | tf_op jit(solution)/shard_map/ppermute | solution.py:31
  816.6 25.2 %collective-permute-done.27 = f32[128,2560]{1,0:T(8,128)S(1)} collective-permute-done((f32[128,2560]{1,0:T(8,128)}, f32[128,2560]{1,0:T(8,128)S(1)}, u32[]{:S(2)}, u32[]{:S(2)}) %collective-permute-start.27) | collective-permute-done | bytes 1310752 | tf_op jit(solution)/shard_map/ppermute | solution.py:31
  842.0 29.9 %collective-permute-done.28 = f32[128,2560]{1,0:T(8,128)S(1)} collective-permute-done((f32[128,2560]{1,0:T(8,128)}, f32[128,2560]{1,0:T(8,128)S(1)}, u32[]{:S(2)}, u32[]{:S(2)}) %collective-permute-start.28) | collective-permute-done | bytes 1310752 | tf_op jit(solution)/shard_map/ppermute | solution.py:31
  874.1 4.1 copy-done.5
  (185 shorter events, 81.7 us)
Async XLA Ops:
  6.5 130.4 %all-reduce.13.cloned.1.call-start = ((), (), s32[]{:S(2)}) async-start(), calls=%async_computation | async-start | bytes 524288 | tf_op jit(solution)/shard_map/psum | solution.py:282
  21.5 59.3 %collective-permute-start = (f32[256,2560]{1,0:T(8,128)}, f32[256,2560]{1,0:T(8,128)}, u32[]{:S(2)}, u32[]{:S(2)}) collective-permute-start(f32[256,2560]{1,0:T(8,128)} %get-tuple-element.77), channel_id=1, source_target_pairs={{0,1},{1,0},{2,3},{3,2},{4,5},{5,4},{6,7},{7,6},{8,9},{9,8},{10,11... | collective-permute-start | bytes 7864328 | tf_op jit(solution)/shard_map/ppermute | solution.py:31
  23.1 177.7 %collective-permute-start.1 = (f32[256,2560]{1,0:T(8,128)}, f32[256,2560]{1,0:T(8,128)}, u32[]{:S(2)}, u32[]{:S(2)}) collective-permute-start(f32[256,2560]{1,0:T(8,128)} %get-tuple-element.75), channel_id=1, source_target_pairs={{0,2},{1,3},{2,0},{3,1},{4,6},{5,7},{6,4},{7,5},{8,10},{9,11},{10,... | collective-permute-start | bytes 7864328 | tf_op jit(solution)/shard_map/ppermute | solution.py:31
  23.6 494.1 %collective-permute-start.2 = (f32[256,2560]{1,0:T(8,128)}, f32[256,2560]{1,0:T(8,128)}, u32[]{:S(2)}, u32[]{:S(2)}) collective-permute-start(f32[256,2560]{1,0:T(8,128)} %get-tuple-element.74), channel_id=1, source_target_pairs={{0,3},{1,2},{2,1},{3,0},{4,7},{5,6},{6,5},{7,4},{8,11},{9,10},{10,... | collective-permute-start | bytes 7864328 | tf_op jit(solution)/shard_map/ppermute | solution.py:31
  25.1 492.5 %collective-permute-start.3 = (f32[256,2560]{1,0:T(8,128)}, f32[256,2560]{1,0:T(8,128)}, u32[]{:S(2)}, u32[]{:S(2)}) collective-permute-start(f32[256,2560]{1,0:T(8,128)} %get-tuple-element.73), channel_id=1, source_target_pairs={{0,4},{1,5},{2,6},{3,7},{4,0},{5,1},{6,2},{7,3},{8,12},{9,13},{10,... | collective-permute-start | bytes 7864328 | tf_op jit(solution)/shard_map/ppermute | solution.py:31
  27.7 490.0 %collective-permute-start.4 = (f32[256,2560]{1,0:T(8,128)}, f32[256,2560]{1,0:T(8,128)}, u32[]{:S(2)}, u32[]{:S(2)}) collective-permute-start(f32[256,2560]{1,0:T(8,128)} %get-tuple-element.72), channel_id=1, source_target_pairs={{0,5},{1,4},{2,7},{3,6},{4,1},{5,0},{6,3},{7,2},{8,13},{9,12},{10,... | collective-permute-start | bytes 7864328 | tf_op jit(solution)/shard_map/ppermute | solution.py:31
  80.8 436.8 %collective-permute-start.5 = (f32[256,2560]{1,0:T(8,128)}, f32[256,2560]{1,0:T(8,128)}, u32[]{:S(2)}, u32[]{:S(2)}) collective-permute-start(f32[256,2560]{1,0:T(8,128)} %get-tuple-element.78), channel_id=1, source_target_pairs={{0,6},{1,7},{2,4},{3,5},{4,2},{5,3},{6,0},{7,1},{8,14},{9,15},{10,... | collective-permute-start | bytes 7864328 | tf_op jit(solution)/shard_map/ppermute | solution.py:31
  104.9 412.7 %all-reduce.15.cloned.1.call-start = ((), (), s32[]{:S(2)}) async-start(), calls=%async_computation.1 | async-start | bytes 524288 | tf_op jit(solution)/shard_map/psum | solution.py:283
  200.8 316.9 %collective-permute-start.6 = (f32[256,2560]{1,0:T(8,128)}, f32[256,2560]{1,0:T(8,128)}, u32[]{:S(2)}, u32[]{:S(2)}) collective-permute-start(f32[256,2560]{1,0:T(8,128)} %get-tuple-element.71), channel_id=1, source_target_pairs={{0,7},{1,6},{2,5},{3,4},{4,3},{5,2},{6,1},{7,0},{8,15},{9,14},{10,... | collective-permute-start | bytes 7864328 | tf_op jit(solution)/shard_map/ppermute | solution.py:31
  553.2 14.1 %collective-permute-start.8 = (f32[256,512]{1,0:T(8,128)S(1)}, f32[256,512]{1,0:T(8,128)}, u32[]{:S(2)}, u32[]{:S(2)}) collective-permute-start(f32[256,512]{1,0:T(8,128)S(1)} %constant_dynamic-slice_fusion.8), channel_id=1, source_target_pairs={{0,16},{8,24},{16,0},{24,8},{1,17},{9,25},{17,1},{25,9},{2,18},{10... | collective-permute-start | bytes 1572872 | tf_op jit(solution)/shard_map/ppermute | solution.py:31
  569.3 7.4 collective-permute-start.10
  570.8 7.9 collective-permute-start.12
  572.4 8.9 collective-permute-start.13
  575.2 9.1 %collective-permute-start.14 = (f32[32,512]{1,0:T(8,128)}, f32[32,512]{1,0:T(8,128)}, u32[]{:S(2)}, u32[]{:S(2)}) collective-permute-start(f32[32,512]{1,0:T(8,128)} %get-tuple-element.91), channel_id=1, source_target_pairs={{0,6},{1,7},{2,4},{3,5},{4,2},{5,3},{6,0},{7,1},{8,14},{9,15},{10,... | collective-permute-start | bytes 196616 | tf_op jit(solution)/shard_map/ppermute | solution.py:31
  576.8 9.0 %collective-permute-start.15 = (f32[32,512]{1,0:T(8,128)}, f32[32,512]{1,0:T(8,128)}, u32[]{:S(2)}, u32[]{:S(2)}) collective-permute-start(f32[32,512]{1,0:T(8,128)} %get-tuple-element.90), channel_id=1, source_target_pairs={{0,7},{1,6},{2,5},{3,4},{4,3},{5,2},{6,1},{7,0},{8,15},{9,14},{10,... | collective-permute-start | bytes 196616 | tf_op jit(solution)/shard_map/ppermute | solution.py:31
  576.8 9.0 %collective-permute-start.9 = (f32[32,512]{1,0:T(8,128)}, f32[32,512]{1,0:T(8,128)}, u32[]{:S(2)}, u32[]{:S(2)}) collective-permute-start(f32[32,512]{1,0:T(8,128)} %get-tuple-element.89), channel_id=1, source_target_pairs={{0,1},{1,0},{2,3},{3,2},{4,5},{5,4},{6,7},{7,6},{8,9},{9,8},{10,11... | collective-permute-start | bytes 196616 | tf_op jit(solution)/shard_map/ppermute | solution.py:31
  588.2 6.6 collective-permute-start.16
  588.9 7.6 collective-permute-start.17
  588.9 9.9 %collective-permute-start.18 = (f32[32,512]{1,0:T(8,128)S(1)}, f32[32,512]{1,0:T(8,128)S(1)}, u32[]{:S(2)}, u32[]{:S(2)}) collective-permute-start(f32[32,512]{1,0:T(8,128)S(1)} %get-tuple-element.64), channel_id=1, source_target_pairs={{0,3},{1,2},{2,1},{3,0},{4,7},{5,6},{6,5},{7,4},{8,11},{9,10},{10,... | collective-permute-start | bytes 196616 | tf_op jit(solution)/shard_map/ppermute | solution.py:31
  591.7 7.8 collective-permute-start.19
  592.2 7.9 collective-permute-start.20
  594.8 9.0 %collective-permute-start.21 = (f32[32,512]{1,0:T(8,128)S(1)}, f32[32,512]{1,0:T(8,128)S(1)}, u32[]{:S(2)}, u32[]{:S(2)}) collective-permute-start(f32[32,512]{1,0:T(8,128)S(1)} %get-tuple-element.64), channel_id=1, source_target_pairs={{0,6},{1,7},{2,4},{3,5},{4,2},{5,3},{6,0},{7,1},{8,14},{9,15},{10,... | collective-permute-start | bytes 196616 | tf_op jit(solution)/shard_map/ppermute | solution.py:31
  596.5 8.1 collective-permute-start.22
  605.2 13.0 %collective-permute-start.23 = (f32[256,512]{1,0:T(8,128)}, f32[256,512]{1,0:T(8,128)S(1)}, u32[]{:S(2)}, u32[]{:S(2)}) collective-permute-start(f32[256,512]{1,0:T(8,128)} %constant_dynamic-update-slice_fusion.22), channel_id=1, source_target_pairs={{0,16},{8,24},{16,0},{24,8},{1,17},{9,25},{17,1},{25,9},{2,18},{10... | collective-permute-start | bytes 1572872 | tf_op jit(solution)/shard_map/ppermute | solution.py:31
  618.3 8.2 collective-permute-start.24
  643.6 142.0 %collective-permute-start.25 = (f32[128,2560]{1,0:T(8,128)}, f32[128,2560]{1,0:T(8,128)S(1)}, u32[]{:S(2)}, u32[]{:S(2)}) collective-permute-start(f32[128,2560]{1,0:T(8,128)} %get-tuple-element.27), channel_id=1, source_target_pairs={{0,4},{1,5},{2,6},{3,7},{4,0},{5,1},{6,2},{7,3},{8,12},{9,13},{10,... | collective-permute-start | bytes 3932168 | tf_op jit(solution)/shard_map/ppermute | solution.py:31
  643.8 171.7 %collective-permute-start.26 = (f32[128,2560]{1,0:T(8,128)}, f32[128,2560]{1,0:T(8,128)S(1)}, u32[]{:S(2)}, u32[]{:S(2)}) collective-permute-start(f32[128,2560]{1,0:T(8,128)} %get-tuple-element.28), channel_id=1, source_target_pairs={{0,6},{1,7},{2,4},{3,5},{4,2},{5,3},{6,0},{7,1},{8,14},{9,15},{10,... | collective-permute-start | bytes 3932168 | tf_op jit(solution)/shard_map/ppermute | solution.py:31
  645.2 196.7 %collective-permute-start.27 = (f32[128,2560]{1,0:T(8,128)}, f32[128,2560]{1,0:T(8,128)S(1)}, u32[]{:S(2)}, u32[]{:S(2)}) collective-permute-start(f32[128,2560]{1,0:T(8,128)} %get-tuple-element.29), channel_id=1, source_target_pairs={{0,5},{1,4},{2,7},{3,6},{4,1},{5,0},{6,3},{7,2},{8,13},{9,12},{10,... | collective-permute-start | bytes 3932168 | tf_op jit(solution)/shard_map/ppermute | solution.py:31
  648.9 222.9 %collective-permute-start.28 = (f32[128,2560]{1,0:T(8,128)}, f32[128,2560]{1,0:T(8,128)S(1)}, u32[]{:S(2)}, u32[]{:S(2)}) collective-permute-start(f32[128,2560]{1,0:T(8,128)} %get-tuple-element.30), channel_id=1, source_target_pairs={{0,7},{1,6},{2,5},{3,4},{4,3},{5,2},{6,1},{7,0},{8,15},{9,14},{10,... | collective-permute-start | bytes 3932168 | tf_op jit(solution)/shard_map/ppermute | solution.py:31
  650.4 221.6 %collective-permute-start.29 = (f32[128,2560]{1,0:T(8,128)}, f32[128,2560]{1,0:T(8,128)S(1)}, u32[]{:S(2)}, u32[]{:S(2)}) collective-permute-start(f32[128,2560]{1,0:T(8,128)} %get-tuple-element.31), channel_id=1, source_target_pairs={{0,2},{1,3},{2,0},{3,1},{4,6},{5,7},{6,4},{7,5},{8,10},{9,11},{10,... | collective-permute-start | bytes 3932168 | tf_op jit(solution)/shard_map/ppermute | solution.py:31
  785.6 86.5 %collective-permute-start.30 = (f32[128,2560]{1,0:T(8,128)}, f32[128,2560]{1,0:T(8,128)S(1)}, u32[]{:S(2)}, u32[]{:S(2)}) collective-permute-start(f32[128,2560]{1,0:T(8,128)} %get-tuple-element.32), channel_id=1, source_target_pairs={{0,3},{1,2},{2,1},{3,0},{4,7},{5,6},{6,5},{7,4},{8,11},{9,10},{10,... | collective-permute-start | bytes 3932168 | tf_op jit(solution)/shard_map/ppermute | solution.py:31
  815.4 58.5 %collective-permute-start.31 = (f32[128,2560]{1,0:T(8,128)S(1)}, f32[128,2560]{1,0:T(8,128)S(1)}, u32[]{:S(2)}, u32[]{:S(2)}) collective-permute-start(f32[128,2560]{1,0:T(8,128)S(1)} %copy-done.14), channel_id=1, source_target_pairs={{0,1},{1,0},{2,3},{3,2},{4,5},{5,4},{6,7},{7,6},{8,9},{9,8},{10,11... | collective-permute-start | bytes 3932168 | tf_op jit(solution)/shard_map/ppermute | solution.py:31
  (17 other events, 800.1 us)
Sparse Core Ops, SparseCore 0:
  105.0 31.8 all-reduce.12
  143.3 337.2 all-reduce.14
